TPU v7x, 128 devices: a whole 4x4x4 slice. The times are simulated.
128 devices in a mesh: ctx: 16 (over z, y), tp: 8 (over x, core).
Axes of the slice: x: 4, y: 4, z: 4, core: 2. Of those that a mesh axis runs over, the one named last changes fastest.
Arguments:
- queries: bfloat16 [16384, 2048], P('ctx', 'tp'), may hold values from -6 to 6
- keys: bfloat16 [16384, 2048], P('ctx', 'tp'), may hold values from -6 to 6
- values: bfloat16 [16384, 4096], P('ctx', 'tp'), may hold values from -6 to 6
- grad_out: bfloat16 [16384, 4096], P('ctx', 'tp'), may hold values from -6 to 6
- input_gate: float32 [8, 16384], P('tp', 'ctx'), may hold values from -6 to 260
- forget_gate: float32 [8, 16384], P('tp', 'ctx'), may hold values from 0 to 12
- query_weight: bfloat16 [4096, 2048], P(None, 'tp'), may hold values from -0.09375 to 0.09375
- key_weight: bfloat16 [4096, 2048], P(None, 'tp'), may hold values from -0.09375 to 0.09375
- value_weight: bfloat16 [4096, 4096], P(None, 'tp'), may hold values from -0.09375 to 0.09375
Outputs:
- token_grad: bfloat16 [16384, 4096], P(('ctx', 'tp'))
- input_gate_grad: float32 [8, 16384], P('tp', 'ctx')
- forget_gate_grad: float32 [8, 16384], P('tp', 'ctx')
All inputs are finite; a program needn't handle non-finite values.
Results may differ from a plain program's by a relative error of at most 0.035.
Values may be sent and summed in bfloat16 or wider, within the bound.
A program may use at most 128 MiB of HBM per device.

v0:
```python
import math

import jax
import jax.numpy as jnp
from jax import lax
from jax.sharding import PartitionSpec as P

HIGH = lax.Precision.HIGHEST
FLOOR = -1e30


def carried_in(shard, axis, combine, identity, reverse):
    length, index = (lax.axis_size(axis), lax.axis_index(axis))
    everything = jax.tree.map(lambda part: lax.all_gather(part, axis), shard)
    start = jax.tree.map(
        lambda part, zero: jnp.broadcast_to(jnp.asarray(zero, part.dtype), part.shape),
        shard,
        identity,
    )

    def hop(k, before):
        at = length - 1 - k if reverse else k
        reached = at > index if reverse else at < index
        new = combine(before, jax.tree.map(lambda part: part[at], everything))
        return jax.tree.map(lambda a, b: jnp.where(reached, a, b), new, before)

    return lax.fori_loop(0, length, hop, start)


def join_states(earlier, later):
    early_state, early_norm, early_peak, early_total = earlier
    late_state, late_norm, late_peak, late_total = later
    shifted = early_peak + late_total
    peak = jnp.maximum(shifted, late_peak)
    old_scale = jnp.exp(shifted - peak)
    new_scale = jnp.exp(late_peak - peak)
    state = old_scale[..., None, None] * early_state + new_scale[..., None, None] * late_state
    norm_vec = old_scale[..., None] * early_norm + new_scale[..., None] * late_norm
    return (state, norm_vec, peak, early_total + late_total)


def own_summary(keys, values, input_gate, forget_gate):
    log_forget = jax.nn.log_sigmoid(forget_gate)
    cumulative = jnp.cumsum(log_forget)
    block_total = cumulative[-1]
    own_log = block_total - cumulative + input_gate
    own_peak = jnp.max(own_log)
    lifted = jnp.exp(own_log - own_peak)
    key_wide = keys.astype(jnp.float32)
    value_wide = values.astype(jnp.float32)
    local_state = jnp.dot((value_wide * lifted[:, None]).T, key_wide, precision=HIGH)
    local_norm = jnp.dot(lifted, key_wide, precision=HIGH)
    return (local_state, local_norm, own_peak, block_total, cumulative, own_log)


def read_out(
    queries,
    keys,
    values,
    grad_out,
    input_gate,
    cumulative,
    previous_state,
    previous_norm,
    previous_peak,
):
    length = queries.shape[0]
    shrink = 1.0 / math.sqrt(queries.shape[1])
    positions = jnp.arange(length)
    causal = positions[:, None] >= positions[None, :]
    log_decay = jnp.where(
        causal, cumulative[:, None] - cumulative[None, :] + input_gate[None, :], FLOOR
    )
    stabilizer = jnp.maximum(jnp.max(log_decay, axis=1), cumulative + previous_peak)
    damping = jnp.where(causal, jnp.exp(log_decay - stabilizer[:, None]), 0.0)
    scores = jnp.dot(queries, keys.T, preferred_element_type=jnp.float32) * shrink
    weights = damping * scores
    weights_low = weights.astype(jnp.bfloat16)
    carried_scale = jnp.exp(cumulative + previous_peak - stabilizer)
    query_wide = queries.astype(jnp.float32)
    carried = jnp.dot(query_wide, previous_state.T, precision=HIGH) * shrink
    carried_norm = jnp.dot(query_wide, previous_norm, precision=HIGH) * shrink
    numerator = (
        jnp.dot(weights_low, values, preferred_element_type=jnp.float32)
        + carried_scale[:, None] * carried
    )
    denominator = jnp.sum(weights, axis=1) + carried_scale * carried_norm
    divisor = jnp.sqrt(denominator * denominator + 1.0)
    output = numerator / divisor[:, None]
    upstream = grad_out.astype(jnp.float32)
    grad_numerator = upstream / divisor[:, None]
    grad_denominator = -jnp.sum(upstream * output, axis=1) * denominator / (divisor * divisor)
    exponent = cumulative - stabilizer
    grad_peak = jnp.max(exponent)
    lifted = jnp.exp(exponent - grad_peak)
    grad_state = jnp.dot((grad_numerator * lifted[:, None]).T, query_wide, precision=HIGH) * shrink
    grad_norm = jnp.dot(grad_denominator * lifted, query_wide, precision=HIGH) * shrink
    saved = (
        damping,
        weights,
        weights_low,
        carried_scale,
        carried,
        carried_norm,
        grad_numerator,
        grad_denominator,
    )
    return (grad_state, grad_norm, grad_peak, saved)


def pull_back(
    queries,
    keys,
    values,
    forget_gate,
    own_log,
    block_total,
    own_peak,
    local_state,
    local_norm,
    previous_state,
    previous_norm,
    previous_peak,
    after_state,
    after_norm,
    after_peak,
    saved,
):
    (
        damping,
        weights,
        weights_low,
        carried_scale,
        carried,
        carried_norm,
        grad_numerator,
        grad_denominator,
    ) = saved
    shrink = 1.0 / math.sqrt(queries.shape[1])
    grad_low = grad_numerator.astype(jnp.bfloat16)
    pair_grad = (
        jnp.dot(grad_low, values.T, preferred_element_type=jnp.float32) + grad_denominator[:, None]
    )
    score_grad = damping * pair_grad
    log_grad = weights * pair_grad
    score_low = score_grad.astype(jnp.bfloat16)
    key_wide = keys.astype(jnp.float32)
    value_wide = values.astype(jnp.float32)
    reaching = jnp.exp(own_log + after_peak)
    pulled = jnp.dot(key_wide, after_state.T, precision=HIGH)
    carried_back = (
        jnp.dot(grad_numerator, previous_state, precision=HIGH)
        + grad_denominator[:, None] * previous_norm[None, :]
    )
    query_grad = (
        jnp.dot(score_low, keys, preferred_element_type=jnp.float32)
        + carried_scale[:, None] * carried_back
    ) * shrink
    key_grad = jnp.dot(score_low.T, queries, preferred_element_type=jnp.float32) * shrink
    key_grad = key_grad + reaching[:, None] * (
        jnp.dot(value_wide, after_state, precision=HIGH) + after_norm[None, :]
    )
    value_grad = (
        jnp.dot(weights_low.T, grad_low, preferred_element_type=jnp.float32)
        + reaching[:, None] * pulled
    )
    input_grad = jnp.sum(log_grad, axis=0) + reaching * (
        jnp.sum(value_wide * pulled, axis=1) + jnp.dot(key_wide, after_norm, precision=HIGH)
    )
    row_grad = jnp.sum(log_grad, axis=1) + carried_scale * (
        jnp.sum(grad_numerator * carried, axis=1) + grad_denominator * carried_norm
    )
    end_peak = jnp.maximum(previous_peak + block_total, own_peak)
    old_scale = jnp.exp(previous_peak + block_total - end_peak)
    new_scale = jnp.exp(own_peak - end_peak)
    end_state = old_scale * previous_state + new_scale * local_state
    end_norm = old_scale * previous_norm + new_scale * local_norm
    link_grad = jnp.exp(end_peak + after_peak) * (
        jnp.sum(after_state * end_state) + jnp.sum(after_norm * end_norm)
    )
    balance = row_grad - input_grad
    forget_log_grad = jnp.flip(jnp.cumsum(jnp.flip(balance))) + link_grad
    forget_grad = forget_log_grad * jax.nn.sigmoid(-forget_gate)
    return (
        query_grad.astype(jnp.bfloat16),
        key_grad.astype(jnp.bfloat16),
        value_grad.astype(jnp.bfloat16),
        input_grad,
        forget_grad,
    )


def split_heads(array, heads, size):
    return array.reshape(array.shape[0], heads, size).transpose(1, 0, 2)


def on_device(
    queries, keys, values, grad_out, input_gate, forget_gate, query_weight, key_weight, value_weight
):
    heads = input_gate.shape[0]
    depth = queries.shape[1] // heads
    breadth = values.shape[1] // heads
    query_heads = split_heads(queries, heads, depth)
    key_heads = split_heads(keys, heads, depth)
    value_heads = split_heads(values, heads, breadth)
    grad_heads = split_heads(grad_out, heads, breadth)
    local_state, local_norm, own_peak, block_total, cumulative, own_log = jax.vmap(own_summary)(
        key_heads, value_heads, input_gate, forget_gate
    )
    empty_state = jnp.zeros_like(local_state)
    empty_norm = jnp.zeros_like(local_norm)
    lowest = jnp.full_like(own_peak, FLOOR)
    nothing = jnp.zeros_like(block_total)
    previous_state, previous_norm, previous_peak, spent = carried_in(
        (local_state, local_norm, own_peak, block_total),
        "ctx",
        join_states,
        (empty_state, empty_norm, lowest, nothing),
        False,
    )
    grad_state, grad_norm, grad_peak, saved = jax.vmap(read_out)(
        query_heads,
        key_heads,
        value_heads,
        grad_heads,
        input_gate,
        cumulative,
        previous_state,
        previous_norm,
        previous_peak,
    )
    after_state, after_norm, after_peak, spent_back = carried_in(
        (grad_state, grad_norm, grad_peak, block_total),
        "ctx",
        join_states,
        (empty_state, empty_norm, lowest, nothing),
        True,
    )
    query_low, key_low, value_low, input_grad, forget_grad = jax.vmap(pull_back)(
        query_heads,
        key_heads,
        value_heads,
        forget_gate,
        own_log,
        block_total,
        own_peak,
        local_state,
        local_norm,
        previous_state,
        previous_norm,
        previous_peak,
        after_state,
        after_norm,
        after_peak,
        saved,
    )
    width = query_weight.shape[0]
    query_cols = query_weight.reshape(width, heads, depth)
    key_cols = key_weight.reshape(width, heads, depth)
    value_cols = value_weight.reshape(width, heads, breadth)
    term = jnp.einsum("htk,ehk->the", query_low, query_cols, preferred_element_type=jnp.float32)
    term = term + jnp.einsum("htk,ehk->the", key_low, key_cols, preferred_element_type=jnp.float32)
    term = term + jnp.einsum(
        "htk,ehk->the", value_low, value_cols, preferred_element_type=jnp.float32
    )
    summed = lax.psum_scatter(
        term.astype(jnp.bfloat16), "tp", scatter_dimension=0, tiled=True
    ).astype(jnp.float32)
    token_grad = jnp.sum(summed, axis=1).astype(jnp.bfloat16)
    return (token_grad, input_grad, forget_grad)


def solution(mesh):
    placed = (
        P("ctx", "tp"),
        P("ctx", "tp"),
        P("ctx", "tp"),
        P("ctx", "tp"),
        P("tp", "ctx"),
        P("tp", "ctx"),
        P(None, "tp"),
        P(None, "tp"),
        P(None, "tp"),
    )
    return jax.shard_map(
        on_device,
        mesh=mesh,
        in_specs=placed,
        out_specs=(P(("ctx", "tp"), None), P("tp", "ctx"), P("tp", "ctx")),
        check_vma=False,
    )
```

profile of v0, /device:TPU:1, one launch (start us, length us, event | category | flops | bytes accessed | tf_op | source)
XLA Modules:
  0.0 403.8 jit_solution(7715344119866133881)
XLA Ops:
  7.3 0.9 fusion.46
  9.5 2.0 fusion.57
  12.2 4.1 %fusion.3 = f32[512,256]{1,0:T(8,128)} fusion(bf16[1024,256]{1,0:T(8,128)(2,1)} %param.14, bf16[1024,512]{1,0:T(8,128)(2,1)} %param.15, f32[1024]{0:T(1024)S(1)} %bitcast.228), kind=kOutput, calls=%fused_computation.27 | convolution fusion | flops 1611661312 | bytes 2101248 | tf_op jit(solution)/shard_map/vmap()/dot_general | solution.py:51
  16.4 1.3 dynamic-slice
  17.7 1.3 bitcast_dynamic-update-slice_fusion
  19.0 1.4 dynamic-update-slice.1
  20.4 35.7 %all-reduce.3 = (f32[16]{0:T(128)S(1)}, f32[16]{0:T(128)S(1)}) all-reduce(f32[16]{0:T(128)S(1)} %bitcast_dynamic-update-slice_fusion, f32[16]{0:T(128)S(1)} %dynamic-update-slice.1), channel_id=1, replica_groups=mesh['ctx'=16,'tp'=8] {'ctx'}, use_global_device_ids=true, to_apply=%add | all-reduce | flops 32 | bytes 256
  56.1 2.3 copy.29
  58.7 16.8 %all-gather.4 = f32[16,1,256]{2,1,0:T(1,128)S(1)} all-gather(f32[1,1,256]{2,1,0:T(1,128)S(1)} %bitcast.237), channel_id=3, replica_groups=mesh['ctx'=16,'tp'=8] {'ctx'}, dimensions={0}, use_global_device_ids=true | all-gather | bytes 17408 | tf_op jit(solution)/shard_map/all_gather | solution.py:14
  76.1 14.8 %all-gather.9.cloned.1.call-done = f32[8192,256]{1,0:T(8,128)} async-done(((f32[512,256]{1,0:T(8,128)}), f32[8192,256]{1,0:T(8,128)}) %all-gather.9.cloned.1.call-update) | async-done | bytes 8388624 | tf_op jit(solution)/shard_map/all_gather | solution.py:14
  90.9 66.2 %while.38 = (s32[]{:T(128)}, f32[1,512,256]{2,1,0:T(8,128)S(1)}, f32[1,256]{1,0:T(1,128)S(1)}, f32[1]{0:T(128)}, s32[]{:T(128)}, /*index=5*/f32[16,1]{0,1:T(1,12...) while((s32[]{:T(128)}, f32[1,512,256]{2,1,0:T(8,128)S(1)}, ...), condition=%wide.region_5.6_spmd.clone, body=%wide.region_4.5_spmd.clone.sunk | while | flops 656649 | bytes 1576196 | solution.py:27
  93.6 1.4 fusion.85
  97.7 1.4 fusion.85
  101.9 1.4 fusion.85
  106.0 1.4 fusion.85
  110.2 1.4 fusion.85
  114.3 1.4 fusion.85
  118.4 1.4 fusion.85
  122.6 1.4 fusion.85
  126.7 1.4 fusion.85
  130.8 1.4 fusion.85
  135.0 1.4 fusion.85
  139.1 1.4 fusion.85
  143.2 1.4 fusion.85
  147.4 1.4 fusion.85
  151.5 1.4 fusion.85
  155.6 1.4 fusion.85
  157.8 1.5 fusion.53
  159.3 2.3 fusion.58
  161.7 1.3 fusion.6
  163.7 1.5 fusion.5
  165.8 2.1 fusion.22
  168.0 1.3 dynamic-update-slice.2
  169.3 31.6 %all-reduce.2 = f32[16]{0:T(128)S(1)} all-reduce(f32[16]{0:T(128)S(1)} %dynamic-update-slice.2), channel_id=1, replica_groups=mesh['ctx'=16,'tp'=8] {'ctx'}, use_global_device_ids=true, to_apply=%add.2 | all-reduce | flops 16 | bytes 128
  200.9 1.5 fusion.61
  202.4 17.0 %all-gather.5 = f32[16,1,256]{2,1,0:T(1,128)S(1)} all-gather(f32[1,1,256]{2,1,0:T(1,128)S(1)} %bitcast.241), channel_id=5, replica_groups=mesh['ctx'=16,'tp'=8] {'ctx'}, dimensions={0}, use_global_device_ids=true | all-gather | bytes 17408 | tf_op jit(solution)/shard_map/all_gather | solution.py:14
  219.4 4.9 %fusion.12 = (f32[1024]{0:T(1024)S(1)}, f32[1024]{0:T(1024)S(1)}, bf16[1024,1024]{0,1:T(8,128)(2,1)S(1)}) fusion(f32[1024,1024]{0,1:T(8,128)} %copy-done.14, f32[1024]{0:T(1024)S(1)} %get-tuple-element.563, f32[1024]{0:T(1024)S(1)} %get-tuple-element.567, f32[1024]{0:T(1024)S(1)} %bitcast.244, f32[1024]{0:T(1024)S(1)} %bitcast_add_fusion.6, ...), kind=kOutput, calls=%fused_computation.39 | convolution fusion | flops 1087895552 | bytes 8417280 | tf_op jit(solution)/shard_map/vmap()/dot_general | solution.py:142
  224.3 1.8 convolution_multiply_fusion
  226.1 0.8 fusion.59
  227.3 3.6 fusion.20
  231.0 8.1 %fusion.60 = f32[1024,4096]{1,0:T(8,128)} fusion(bf16[1024,256]{1,0:T(8,128)(2,1)S(1)} %fusion.20, bf16[4096,256]{1,0:T(8,128)(2,1)S(1)} %copy-done), kind=kOutput, calls=%fused_computation.110 | convolution fusion | flops 2147483648 | bytes 19398656 | tf_op jit(solution)/shard_map/htk,ehk->the/dot_general | solution.py:261
  239.1 63.1 %while.39 = (s32[]{:T(128)}, f32[1,512,256]{2,1,0:T(8,128)S(1)}, f32[1,256]{1,0:T(1,128)S(1)}, f32[1]{0:T(128)}, s32[]{:T(128)}, /*index=5*/f32[16,1]{0,1:T(1,12...) while((s32[]{:T(128)}, f32[1,512,256]{2,1,0:T(8,128)S(1)}, ...), condition=%wide.region_10.11_spmd.clone, body=%wide.region_9.10_spmd.clone.sunk | while | flops 656653 | bytes 1576258 | solution.py:27
  241.6 1.4 fusion.86
  245.5 1.4 fusion.86
  249.4 1.4 fusion.86
  253.4 1.4 fusion.86
  257.3 1.4 fusion.86
  261.3 1.4 fusion.86
  265.2 1.4 fusion.86
  269.2 1.4 fusion.86
  273.1 1.4 fusion.86
  277.1 1.4 fusion.86
  281.0 1.4 fusion.86
  285.0 1.4 fusion.86
  288.9 1.4 fusion.86
  292.9 1.4 fusion.86
  296.8 1.4 fusion.86
  300.8 1.4 fusion.86
  302.8 2.5 fusion.4
  305.8 1.1 fusion.21
  306.9 12.6 %fusion.32 = f32[1024,4096]{1,0:T(8,128)} fusion(bf16[4096,512]{1,0:T(8,128)(2,1)} %param.21, f32[512,1024]{0,1:T(8,128)} %get-tuple-element.580, f32[1024]{0:T(1024)S(1)} %bitcast.226, f32[1024,1024]{0,1:T(8,128)} %copy-done.14, bf16[1024,512]{0,1:T(8,128)(2,1)} %copy.29, f32[1024]{0:T(1024)S(1)} %add_sqrt_fusion), kind=kOutput, calls=%fused_computation.59 | convolution fusion | flops 5372903424 | bytes 28319744 | tf_op jit(solution)/shard_map/htk,ehk->the/dot_general | solution.py:263
  319.5 15.9 %fusion.2 = bf16[1024,1,4096]{2,0,1:T(8,128)(2,1)} fusion(f32[1024,4096]{1,0:T(8,128)} %fusion.32, f32[1024,4096]{1,0:T(8,128)} %fusion.60, bf16[1024,256]{1,0:T(8,128)(2,1)S(1)} %fusion.21, bf16[4096,256]{1,0:T(8,128)(2,1)} %param.20), kind=kOutput, calls=%fused_computation.15 | convolution fusion | flops 2160066560 | bytes 44564480 | tf_op jit(solution)/shard_map/htk,ehk->the/dot_general | solution.py:262
  340.4 1.9 fusion.36
  344.1 53.1 %reduce-scatter.2.cloned.1.call-done = bf16[128,1,4096]{2,0,1:T(8,128)(2,1)} async-done(((bf16[1024,1,4096]{2,0,1:T(8,128)(2,1)}), bf16[128,1,4096]{2,0,1:T(8,128)(2,1)}) %reduce-scatter.2.cloned.1.call-update) | async-done | bytes 1048592 | tf_op jit(solution)/shard_map/reduce_scatter | solution.py:266
  (139 shorter events, 31.1 us)
Async XLA Ops:
  7.2 223.8 %copy-start = (bf16[4096,256]{1,0:T(8,128)(2,1)S(1)}, bf16[4096,256]{1,0:T(8,128)(2,1)}, u32[]{:S(2)}) copy-start(bf16[4096,256]{1,0:T(8,128)(2,1)} %param.19) | copy-start | bytes 6291460
  7.2 68.4 %copy-start.13 = (f32[1,1024]{1,0:T(1,128)S(1)}, f32[1,1024]{1,0:T(1,128)}, u32[]{:S(2)}) copy-start(f32[1,1024]{1,0:T(1,128)} %param.17) | copy-start | bytes 12292
  7.2 51.2 %copy-start.2 = (bf16[1024,256]{1,0:T(8,128)(2,1)S(1)}, bf16[1024,256]{1,0:T(8,128)(2,1)}, u32[]{:S(2)}) copy-start(bf16[1024,256]{1,0:T(8,128)(2,1)} %param.14) | copy-start | bytes 1572868
  7.2 83.7 %all-gather.9.cloned.1.call-start = ((), (), s32[]{:S(2)}) async-start(), calls=%async_computation.2 | async-start | bytes 8912896 | tf_op jit(solution)/shard_map/all_gather | solution.py:14
  16.4 222.7 %all-gather.11.cloned.1.call-start = ((), (), s32[]{:S(2)}) async-start(), calls=%async_computation.3 | async-start | bytes 8912896 | tf_op jit(solution)/shard_map/all_gather | solution.py:14
  159.3 2.3 copy-start.7
  159.3 2.3 copy-start.10
  161.6 2.0 copy-start.14
  161.7 2.0 copy-start.5
  167.9 229.4 %reduce-scatter.2.cloned.1.call-start = ((), (), s32[]{:S(2)}) async-start(), calls=%async_computation.1 | async-start | bytes 9437184 | tf_op jit(solution)/shard_map/reduce_scatter | solution.py:266
  219.4 4.9 %copy-start.8 = (bf16[1024,256]{1,0:T(8,128)(2,1)S(1)}, bf16[1024,256]{1,0:T(8,128)(2,1)}, u32[]{:S(2)}) copy-start(bf16[1024,256]{1,0:T(8,128)(2,1)} %param.13) | copy-start | bytes 1572868
  224.3 1.8 copy-start.3
  226.1 1.2 copy-start.11
  239.1 63.2 %copy-start.4 = (bf16[1024,256]{1,0:T(8,128)(2,1)S(1)}, bf16[1024,256]{1,0:T(8,128)(2,1)}, u32[]{:S(2)}) copy-start(bf16[1024,256]{1,0:T(8,128)(2,1)} %param.14) | copy-start | bytes 1572868
  239.1 63.7 %copy-start.6 = (bf16[1024,512]{1,0:T(8,128)(2,1)S(1)}, bf16[1024,512]{1,0:T(8,128)(2,1)}, u32[]{:S(2)}) copy-start(bf16[1024,512]{1,0:T(8,128)(2,1)} %param.15) | copy-start | bytes 3145732
  302.2 3.6 copy-start.9
  335.4 61.9 %copy-start.1 = (bf16[4096,256]{1,0:T(8,128)(2,1)S(1)}, bf16[4096,256]{1,0:T(8,128)(2,1)}, u32[]{:S(2)}) copy-start(bf16[4096,256]{1,0:T(8,128)(2,1)} %param.19) | copy-start | bytes 6291460
  335.4 8.1 %copy-start.12 = (f32[1,1024]{1,0:T(1,128)S(1)}, f32[1,1024]{1,0:T(1,128)}, u32[]{:S(2)}) copy-start(f32[1,1024]{1,0:T(1,128)} %param.18) | copy-start | bytes 12292
Sparse Core Ops, SparseCore 0:
  16.5 74.4 all-gather.8
  168.0 70.6 all-gather.10
  335.5 61.6 reduce-scatter.1
where the time goes:
time: 407 us; the launch traced here: 404 us
  blocking collectives  101 us (25%)
  waiting for transfers between devices  68 us (17%)
  matrix products  66.3 us (16%)
  loops' own time  62.3 us (15%)
  other arithmetic  56.8 us (14%)
  local copies, waits for them, and re-layouts  31.7 us (8%)
  between operations  17.5 us (4%)
    unnamed x2, blocking collectives  67.3 us
    another operation x2, loops' own time, carried_in(): return lax.fori_loop(0, length, hop, start)  62.3 us
    reduce_scatter x1, waiting for transfers between devices, on_device(): lax.psum_scatter(term.astype(jnp.bfloat16), 'tp', scatter_dimension=0, ti...  53.1 us
    select_n x64, other arithmetic, hop(): return jax.tree.map(lambda a, b: jnp.where(reached, a, b), new, before)  46.8 us
    all_gather x2, blocking collectives, carried_in(): everything = jax.tree.map(lambda part: lax.all_gather(part, axis), shard)  33.8 us
    dynamic_slice x32, local copies, waits for them, and re-layouts, hop(): new = combine(before, jax.tree.map(lambda part: part[at], everything))  20.3 us
    dot_general x1, matrix products, on_device(): jnp.einsum('htk,ehk->the', key_low, key_cols, preferred_element_type=jnp....  15.9 us
    all_gather x2, waiting for transfers between devices, carried_in(): everything = jax.tree.map(lambda part: lax.all_gather(part, axis), shard)  14.8 us
  transfers between devices with their start and end apart: 3, of which 2 were waited for; matrix products, arithmetic and copies ran while one was open for 9% of the time, Pallas kernels for 0%

commit v1 on v0

v1 whole, which is shorter than its diff:
```python
import functools

import jax
import jax.numpy as jnp
from jax import lax
from jax.experimental import pallas as pl
from jax.experimental.pallas import tpu as pltpu
from jax.sharding import PartitionSpec as P

MESH = pl.DeviceIdType.MESH
HIGH = lax.Precision.HIGHEST
F32 = jnp.float32
BF16 = jnp.bfloat16
FLOOR = -1e30

TOK, DK, DV, WIDTH = 1024, 256, 512, 4096
BLOCKS = 16
PART = DK // BLOCKS
TILE = 256
TILES = TOK // TILE
COLS = 1024
STEPS = 16
HOPS = 12
OWN = TOK // 8


def nn(a, b):
    return lax.dot_general(a, b, (((1,), (0,)), ((), ())), preferred_element_type=F32)


def nt(a, b):
    return lax.dot_general(a, b, (((1,), (1,)), ((), ())), preferred_element_type=F32)


def row_times(row, matrix):
    high = row.astype(BF16).astype(F32)
    middle = (row - high).astype(BF16).astype(F32)
    low = row - high - middle
    at = lax.broadcasted_iota(jnp.int32, (16, row.shape[1]), 0)
    pieces = jnp.where(at == 0, high, jnp.where(at == 1, middle, jnp.where(at == 2, low, 0.0)))
    return jnp.sum(nn(pieces.astype(BF16), matrix), axis=0, keepdims=True)


def twice(a):
    return jnp.concatenate([a, a], axis=1)


def kernel(
    q_hbm, k_hbm, v_hbm, g_hbm, in_ref, forget_ref, wq_hbm, wk_hbm, wv_hbm,
    token_ref, in_grad_ref, forget_grad_ref,
    q, k, v, g, w_all, q_t, k_t, damp, weigh, pair, score_low, weight_low, act,
    fold, row_a, row_b, wide, stat, stat_back, stat_rx, stat_back_rx,
    fwd_a, fwd_b, fwd_peak, fwd_norm, bwd_a, bwd_b, bwd_peak, bwd_norm,
    local, local_low, grad_low, rx_fwd, tx_fwd, before, rx_bwd, tx_bwd, after,
    product, tx_pair, rx_pair, tx_hop, rx_hop,
    load_sem, stat_send, stat_recv, part_send, part_recv,
    pair_send, pair_recv, hop_send, hop_recv,
):
    ctx, tp = lax.axis_index("ctx"), lax.axis_index("tp")
    chip, core = lax.div(tp, 2), lax.rem(tp, 2)

    def each_peer(do):
        lax.fori_loop(1, BLOCKS, lambda d, _: (do(lax.rem(ctx + d, BLOCKS)), 0)[1], 0)

    def neighbour(side):
        return 2 * lax.rem(chip + 1 + 2 * side, 4) + core

    loads = [
        pltpu.make_async_copy(source, target, load_sem.at[i])
        for i, (source, target) in enumerate(
            (
                (k_hbm, k),
                (v_hbm, v),
                (q_hbm, q),
                (g_hbm, g),
                (wq_hbm, w_all.at[:, pl.ds(0, DK)]),
                (wk_hbm, w_all.at[:, pl.ds(DK, DK)]),
                (wv_hbm, w_all.at[:, pl.ds(2 * DK, DV)]),
            )
        )
    ]
    for load in loads:
        load.start()

    barrier = pltpu.get_barrier_semaphore()
    each_peer(
        lambda p: pl.semaphore_signal(barrier, 1, device_id={"ctx": p}, device_id_type=MESH)
    )
    for partner in (2 * chip + 1 - core, neighbour(0), neighbour(1)):
        pl.semaphore_signal(barrier, 1, device_id={"tp": partner}, device_id_type=MESH)

    def to_fold(row):
        for i in range(8):
            fold[i : i + 1, :] = row[:, 128 * i : 128 * i + 128]
        return fold[...]

    def to_row(folded, row_ref):
        fold[...] = folded
        for i in range(8):
            row_ref[:, 128 * i : 128 * i + 128] = fold[i : i + 1, :]
        return row_ref[...]

    lane = lax.broadcasted_iota(jnp.int32, (8, 128), 1)
    line = lax.broadcasted_iota(jnp.int32, (8, 128), 0)
    down = lax.broadcasted_iota(jnp.int32, (128, 128), 0)
    across = lax.broadcasted_iota(jnp.int32, (128, 128), 1)

    forget = forget_ref[...]
    small = jnp.exp(-jnp.abs(forget))
    series = small * (1.0 - small * (0.5 - small * (1.0 / 3.0 - small * 0.25)))
    log_forget = jnp.minimum(forget, 0.0) - jnp.where(
        small < 0.01, series, jnp.log(1.0 + small)
    )
    log_forget = to_fold(log_forget)
    inside = jnp.dot(
        log_forget, (down <= across).astype(F32), precision=HIGH, preferred_element_type=F32
    )
    lines = jnp.broadcast_to(inside[:, 127:128], (8, 128))
    for d in (1, 2, 4):
        lines = lines + jnp.where(line >= d, pltpu.roll(lines, d, 0), 0.0)
    cumulative = inside + jnp.where(line >= 1, pltpu.roll(lines, 1, 0), 0.0)
    total = lines[7:8, 0:1]
    level = to_fold(in_ref[...]) - cumulative
    top = jnp.max(jnp.max(level, axis=1, keepdims=True), axis=0, keepdims=True)
    first = level[0:1, 0:1]
    lift = jnp.exp(to_row(level, row_a) - top)

    loads[0].wait()
    loads[1].wait()
    k_t[...] = k[...].T
    lifted = k_t[...].astype(F32) * lift
    lifted_high = lifted.astype(BF16)
    lifted_low = (lifted - lifted_high.astype(F32)).astype(BF16)
    local[...] = nn(lifted_high, v[...]) + nn(lifted_low, v[...])
    local_low[...] = local[...].astype(BF16)
    stat[...] = jnp.zeros_like(stat)
    stat[0:1, :] = row_times(lift, k[...])
    stat[1:2, :] = jnp.broadcast_to(total + top, (1, DK))
    stat[2:3, :] = jnp.broadcast_to(total, (1, DK))
    stat[3:4, :] = jnp.broadcast_to(first, (1, DK))

    pl.semaphore_wait(barrier, BLOCKS - 1 + 3)

    def rows_of(ref, p):
        return ref.at[pl.ds(pl.multiple_of(p * PART, PART), PART)]

    def stat_copy(p, way, source, target, slot):
        return pltpu.make_async_remote_copy(
            src_ref=source, dst_ref=target.at[slot], send_sem=stat_send.at[way, p],
            recv_sem=stat_recv.at[way, slot], device_id={"ctx": p}, device_id_type=MESH,
        )

    def part_copy(p, way, source, target, slot):
        return pltpu.make_async_remote_copy(
            src_ref=source, dst_ref=target, send_sem=part_send.at[way, p],
            recv_sem=part_recv.at[way, slot], device_id={"ctx": p}, device_id_type=MESH,
        )

    each_peer(lambda p: stat_copy(p, 0, stat, stat_rx, ctx).start())
    each_peer(lambda p: part_copy(p, 0, rows_of(local_low, p), rx_fwd.at[ctx], ctx).start())
    stat_rx[ctx] = stat[...]
    rx_fwd[ctx] = rows_of(local_low, ctx)[...]

    highest = level
    for d in (1, 2, 4, 8, 16, 32, 64):
        highest = jnp.maximum(
            highest, jnp.where(lane >= d, pltpu.roll(highest, d, 1), FLOOR)
        )
    lines = jnp.broadcast_to(highest[:, 127:128], (8, 128))
    for d in (1, 2, 4):
        lines = jnp.maximum(lines, jnp.where(line >= d, pltpu.roll(lines, d, 0), FLOOR))
    highest = jnp.maximum(highest, jnp.where(line >= 1, pltpu.roll(lines, 1, 0), FLOOR))
    peak_row = to_row(highest, row_b)
    for i in range(8):
        wide[128 * i : 128 * i + 128, :] = jnp.broadcast_to(
            row_a[:, 128 * i : 128 * i + 128], (128, 128)
        ).T
    loads[2].wait()
    loads[3].wait()
    q_t[...] = q[...].T * jnp.asarray(0.0625, BF16)

    def span(i):
        return slice(TILE * i, TILE * (i + 1))

    causal = lax.broadcasted_iota(jnp.int32, (TILE, TILE), 0) <= lax.broadcasted_iota(
        jnp.int32, (TILE, TILE), 1
    )

    def read_tiles(j):
        weight_sum = jnp.zeros((1, TILE), F32)
        pair_sum = jnp.zeros((1, TILE), F32)
        for i in range(j + 1):
            scores = nn(k[span(i), :], q_t[:, span(j)])
            pairs = nt(v[span(i), :], g[span(j), :])
            damping = jnp.exp(twice(wide[span(i), :]) - peak_row[:, span(j)])
            if i == j:
                damping = jnp.where(causal, damping, 0.0)
            weights = damping * scores
            weight_sum = weight_sum + jnp.sum(weights, axis=0, keepdims=True)
            pair_sum = pair_sum + jnp.sum(weights * pairs, axis=0, keepdims=True)
            damp[span(i), span(j)] = damping
            weigh[span(i), span(j)] = weights
            pair[span(i), span(j)] = pairs
        return weight_sum, pair_sum

    sums = [read_tiles(0), read_tiles(1)]

    each_peer(lambda p: stat_copy(p, 0, stat, stat_rx, p).wait_recv())

    def peaks_forward(j, peak):
        fwd_peak[j] = peak
        shifted, own = peak + stat_rx[j, 2:3, :], stat_rx[j, 1:2, :]
        later = jnp.maximum(shifted, own)
        fwd_a[j] = jnp.exp(shifted - later)
        fwd_b[j] = jnp.exp(own - later)
        return later

    lax.fori_loop(0, BLOCKS, peaks_forward, jnp.full((1, DK), FLOOR, F32))

    def peaks_backward(step, peak):
        j = BLOCKS - 1 - step
        bwd_peak[j] = peak
        own = -jnp.maximum(stat_rx[j, 3:4, :], fwd_peak[j])
        shifted = peak + stat_rx[j, 2:3, :]
        later = jnp.maximum(shifted, own)
        bwd_a[j] = jnp.exp(shifted - later)
        bwd_b[j] = jnp.exp(own - later)
        return later

    lax.fori_loop(0, BLOCKS, peaks_backward, jnp.full((1, DK), FLOOR, F32))

    each_peer(lambda p: part_copy(p, 0, rows_of(local_low, p), rx_fwd.at[p], p).wait_recv())

    def join_forward(j, carried):
        state, norm = carried
        tx_fwd[j] = state.astype(BF16)
        fwd_norm[j] = norm
        state = twice(fwd_a[j]) * state + twice(fwd_b[j]) * rx_fwd[j].astype(F32)
        return state, fwd_a[j] * norm + fwd_b[j] * stat_rx[j, 0:1, :]

    nothing = (jnp.zeros((PART, DV), F32), jnp.zeros((1, DK), F32))
    lax.fori_loop(0, BLOCKS, join_forward, nothing)
    each_peer(lambda p: part_copy(p, 1, tx_fwd.at[p], rows_of(before, ctx), ctx).start())
    rows_of(before, ctx)[...] = tx_fwd[ctx]

    sums += [read_tiles(2), read_tiles(3)]
    weight_sum = jnp.concatenate([s[0] for s in sums], axis=1)
    pair_sum = jnp.concatenate([s[1] for s in sums], axis=1)
    before_peak = fwd_peak[ctx][:, 0:1]
    before_norm = fwd_norm[ctx]
    stabilizer = jnp.maximum(peak_row, before_peak)
    shrunk = jnp.exp(peak_row - stabilizer)
    carried_scale = jnp.exp(before_peak - stabilizer)
    carried_norm = row_times(before_norm, q_t[...])
    denominator = weight_sum * shrunk + carried_scale * carried_norm
    square = denominator * denominator + 1.0
    inverse = 1.0 / jnp.sqrt(square)

    each_peer(lambda p: part_copy(p, 1, tx_fwd.at[p], rows_of(before, p), p).wait_recv())

    back = nt(before[...], g[...])
    q_wide = q_t[...].astype(F32)
    carried_pair = jnp.sum(back * q_wide, axis=0, keepdims=True)
    inner = (pair_sum * shrunk + carried_scale * carried_pair) * inverse
    grad_denominator = -inner * denominator / square
    lifted_row = jnp.exp(stabilizer[:, 0:1] - stabilizer)
    grad_low[...] = nn((q_wide * (lifted_row * inverse)).astype(BF16), g[...]).astype(BF16)
    stat_back[...] = jnp.zeros_like(stat_back)
    stat_back[0:1, :] = row_times(lifted_row * grad_denominator * 0.0625, q[...])

    each_peer(lambda p: stat_copy(p, 1, stat_back, stat_back_rx, ctx).start())
    each_peer(lambda p: part_copy(p, 2, rows_of(grad_low, p), rx_bwd.at[ctx], ctx).start())
    stat_back_rx[ctx] = stat_back[...]
    rx_bwd[ctx] = rows_of(grad_low, ctx)[...]

    pair_scale = shrunk * inverse
    pair_shift = shrunk * grad_denominator
    for j in range(TILES):
        for i in range(j + 1):
            at = (span(i), span(j))
            score = damp[at] * (pair[at] * pair_scale[:, span(j)] + pair_shift[:, span(j)])
            score_low[at] = score.astype(BF16)
            weight_low[at] = (weigh[at] * pair_scale[:, span(j)]).astype(BF16)

    each_peer(lambda p: stat_copy(p, 1, stat_back, stat_back_rx, p).wait_recv())
    each_peer(lambda p: part_copy(p, 2, rows_of(grad_low, p), rx_bwd.at[p], p).wait_recv())

    def join_backward(step, carried):
        j = BLOCKS - 1 - step
        state, norm = carried
        tx_bwd[j] = state.astype(BF16)
        bwd_norm[j] = norm
        state = twice(bwd_a[j]) * state + twice(bwd_b[j]) * rx_bwd[j].astype(F32)
        return state, bwd_a[j] * norm + bwd_b[j] * stat_back_rx[j, 0:1, :]

    lax.fori_loop(0, BLOCKS, join_backward, nothing)
    each_peer(lambda p: part_copy(p, 3, tx_bwd.at[p], rows_of(after, ctx), ctx).start())
    rows_of(after, ctx)[...] = tx_bwd[ctx]

    norm_column = jnp.broadcast_to(before_norm, (128, DK)).T
    row_sums = []
    for j in range(TILES):
        near = nn(k_t[:, : TILE * (j + 1)], score_low[: TILE * (j + 1), span(j)])
        outer = twice(norm_column) * grad_denominator[:, span(j)]
        query_grad = near + carried_scale[:, span(j)] * (
            back[:, span(j)] * inverse[:, span(j)] + outer
        )
        row_sums.append(jnp.sum(query_grad * q_wide[:, span(j)], axis=0, keepdims=True))
        act[span(j), 0:DK] = (query_grad * 0.0625).T.astype(BF16)
    row_grad = jnp.concatenate(row_sums, axis=1)
    key_near = [
        nn(score_low[span(i), TILE * i :], q[TILE * i :, :]) * 0.0625 for i in range(TILES)
    ]
    value_near = [nn(weight_low[span(i), TILE * i :], g[TILE * i :, :]) for i in range(TILES)]
    end_a, end_b = fwd_a[ctx][:, 0:1], fwd_b[ctx][:, 0:1]
    end_state = end_a * before[...].astype(F32) + end_b * local[...]
    end_norm = end_a * before_norm + end_b * stat[0:1, :]
    after_peak = bwd_peak[ctx][:, 0:1]
    after_norm = bwd_norm[ctx]
    reaching = jnp.exp(wide[...] + (total + after_peak))

    each_peer(lambda p: part_copy(p, 3, tx_bwd.at[p], rows_of(after, p), p).wait_recv())

    for i in range(TILES):
        reach = twice(reaching[span(i), :])
        key_grad = key_near[i] + reach * (nt(v[span(i), :], after[...]) + after_norm)
        act[span(i), DK : 2 * DK] = key_grad.astype(BF16)
        value_grad = value_near[i] + twice(reach) * nn(k[span(i), :], after[...])
        act[span(i), 2 * DK :] = value_grad.astype(BF16)
        both = key_grad * k[span(i), :].astype(F32)
        wide[span(i), :] = both[:, :128] + both[:, 128:]

    for load in loads[4:]:
        load.wait()

    def pair_copy(s):
        return pltpu.make_async_remote_copy(
            src_ref=tx_pair.at[s], dst_ref=rx_pair.at[s], send_sem=pair_send.at[s],
            recv_sem=pair_recv.at[s], device_id={"tp": 2 * chip + 1 - core}, device_id_type=MESH,
        )

    def hop_copy(s):
        return pltpu.make_async_remote_copy(
            src_ref=tx_hop.at[s], dst_ref=rx_hop.at[s], send_sem=hop_send.at[s],
            recv_sem=hop_recv.at[s], device_id={"tp": neighbour(lax.rem(s, 2))},
            device_id_type=MESH,
        )

    def place(s):
        side, part, phase = lax.rem(s, 2), lax.rem(lax.div(s, 2), 2), lax.div(s, 4)
        middle = jnp.where(phase == 1, 1, 0)
        hop = jnp.where(phase == 0, 2, 1 + 2 * side)
        columns = 2 * (side + middle - 2 * side * middle) + part
        last = s >= HOPS
        return jnp.where(last, 0, hop), jnp.where(last, s - HOPS, columns)

    def multiply(s):
        hop, n = place(s)
        rows = pl.ds(pl.multiple_of(lax.rem(chip + hop, 4) * 2 * OWN, 2 * OWN), 2 * OWN)
        slot = lax.rem(s, 2)
        product[slot] = nt(act[rows, :], w_all[pl.ds(pl.multiple_of(n * COLS, COLS), COLS), :])
        other = pl.ds(pl.multiple_of((1 - core) * OWN, OWN), OWN)
        tx_pair[s] = product[slot, other, :].astype(BF16)
        pair_copy(s).start()

    def own_product(s):
        mine = pl.ds(pl.multiple_of(core * OWN, OWN), OWN)
        pair_copy(s).wait_recv()
        return product[lax.rem(s, 2), mine, :] + rx_pair[s].astype(F32)

    def pass_on(s):
        tx_hop[s] = own_product(s).astype(BF16)
        hop_copy(s).start()

    def join_on(s):
        both = own_product(s)
        hop_copy(s - 8).wait_recv()
        tx_hop[s] = (both + rx_hop[s - 8].astype(F32)).astype(BF16)
        hop_copy(s).start()

    def finish(s):
        n = s - HOPS
        half, part = lax.div(n, 2), lax.rem(n, 2)
        both = own_product(s)
        from_left = 8 - 4 * half + 2 * part
        from_right = 5 + 4 * half + 2 * part
        hop_copy(from_left).wait_recv()
        hop_copy(from_right).wait_recv()
        both = both + rx_hop[from_left].astype(F32) + rx_hop[from_right].astype(F32)
        token_ref[:, pl.ds(pl.multiple_of(n * COLS, COLS), COLS)] = both.astype(BF16)

    def run(first_step, last_step, end):
        def body(s, _):
            multiply(s + 1)
            end(s)
            return 0

        lax.fori_loop(first_step, last_step, body, 0)

    multiply(0)
    run(0, 8, pass_on)
    run(8, 12, join_on)

    for i in range(8):
        in_grad_ref[:, 128 * i : 128 * i + 128] = jnp.sum(
            wide[128 * i : 128 * i + 128, :].T, axis=0, keepdims=True
        )
    linked = jnp.sum(
        jnp.sum(end_state * after[...].astype(F32), axis=1, keepdims=True), axis=0, keepdims=True
    ) + jnp.sum(end_norm * after_norm, axis=1, keepdims=True)
    end_peak = jnp.maximum(before_peak + total, total + top)
    link = jnp.exp(end_peak + after_peak) * linked
    balance = to_fold(row_grad - in_grad_ref[...])
    inside = jnp.dot(
        balance, (down >= across).astype(F32), precision=HIGH, preferred_element_type=F32
    )
    lines = jnp.broadcast_to(inside[:, 0:1], (8, 128))
    for d in (1, 2, 4):
        lines = lines + jnp.where(line < 8 - d, pltpu.roll(lines, 8 - d, 0), 0.0)
    later = inside + jnp.where(line < 7, pltpu.roll(lines, 7, 0), 0.0)
    forget_grad_ref[...] = (to_row(later, row_a) + link) / (1.0 + jnp.exp(forget))

    run(12, 15, finish)
    finish(15)

    def sent(p):
        for way, (source, target) in enumerate(((stat, stat_rx), (stat_back, stat_back_rx))):
            stat_copy(p, way, source, target, ctx).wait_send()
        part_copy(p, 0, rows_of(local_low, p), rx_fwd.at[ctx], ctx).wait_send()
        part_copy(p, 1, tx_fwd.at[p], rows_of(before, ctx), ctx).wait_send()
        part_copy(p, 2, rows_of(grad_low, p), rx_bwd.at[ctx], ctx).wait_send()
        part_copy(p, 3, tx_bwd.at[p], rows_of(after, ctx), ctx).wait_send()

    each_peer(sent)
    lax.fori_loop(0, STEPS, lambda s, _: (pair_copy(s).wait_send(), 0)[1], 0)
    lax.fori_loop(0, HOPS, lambda s, _: (hop_copy(s).wait_send(), 0)[1], 0)


def on_device(*arrays):
    vm = pltpu.VMEM
    dma = pltpu.SemaphoreType.DMA
    anywhere = pl.BlockSpec(memory_space=pl.ANY)
    whole = pl.BlockSpec(memory_space=pltpu.VMEM)
    scratch = [
        vm((TOK, DK), BF16), vm((TOK, DK), BF16), vm((TOK, DV), BF16), vm((TOK, DV), BF16),
        vm((WIDTH, 2 * DK + DV), BF16), vm((DK, TOK), BF16), vm((DK, TOK), BF16),
        vm((TOK, TOK), F32), vm((TOK, TOK), F32), vm((TOK, TOK), F32),
        vm((TOK, TOK), BF16), vm((TOK, TOK), BF16), vm((TOK, 2 * DK + DV), BF16),
        vm((8, 128), F32), vm((1, TOK), F32), vm((1, TOK), F32), vm((TOK, 128), F32),
        vm((8, DK), F32), vm((8, DK), F32), vm((BLOCKS, 8, DK), F32), vm((BLOCKS, 8, DK), F32),
        *[vm((BLOCKS, 1, DK), F32) for _ in range(8)],
        vm((DK, DV), F32), vm((DK, DV), BF16), vm((DK, DV), BF16),
        vm((BLOCKS, PART, DV), BF16), vm((BLOCKS, PART, DV), BF16), vm((DK, DV), BF16),
        vm((BLOCKS, PART, DV), BF16), vm((BLOCKS, PART, DV), BF16), vm((DK, DV), BF16),
        vm((2, 2 * OWN, COLS), F32),
        vm((STEPS, OWN, COLS), BF16), vm((STEPS, OWN, COLS), BF16),
        vm((HOPS, OWN, COLS), BF16), vm((HOPS, OWN, COLS), BF16),
        dma((7,)), dma((2, BLOCKS)), dma((2, BLOCKS)), dma((4, BLOCKS)), dma((4, BLOCKS)),
        dma((STEPS,)), dma((STEPS,)), dma((HOPS,)), dma((HOPS,)),
    ]
    return pl.pallas_call(
        kernel,
        out_shape=(
            jax.ShapeDtypeStruct((OWN, WIDTH), BF16),
            jax.ShapeDtypeStruct((1, TOK), F32),
            jax.ShapeDtypeStruct((1, TOK), F32),
        ),
        in_specs=[anywhere] * 4 + [whole] * 2 + [anywhere] * 3,
        out_specs=(whole, whole, whole),
        scratch_shapes=scratch,
        compiler_params=pltpu.CompilerParams(
            collective_id=0, has_side_effects=True, vmem_limit_bytes=60 * 1024 * 1024
        ),
        cost_estimate=pl.CostEstimate(
            flops=16_000_000_000, bytes_accessed=13_000_000, transcendentals=1_000_000
        ),
    )(*arrays)


def solution(mesh):
    block = P("ctx", "tp")
    gate = P("tp", "ctx")
    weight = P(None, "tp")
    return jax.shard_map(
        on_device,
        mesh=mesh,
        in_specs=(block, block, block, block, gate, gate, weight, weight, weight),
        out_specs=(P(("ctx", "tp"), None), gate, gate),
        check_vma=False,
    )
```

time: 407 us -> 85.5 us (0.21)
  blocking collectives: 101 us -> 0 us
  Pallas kernels: 0 us -> 81.2 us
  waiting for transfers between devices: 68 us -> 0 us
  matrix products: 66.3 us -> 0 us
  loops' own time: 62.3 us -> 0 us
  other arithmetic: 56.8 us -> 0 us
  local copies, waits for them, and re-layouts: 31.7 us -> 3.48 us
  between operations: 17.5 us -> 0.66 us
    pallas_call x0 -> x1, Pallas kernels: none -> 81.2 us  [on_device(): pl.pallas_call(kernel, out_shape=(jax.ShapeDtypeStruct((OWN, WIDTH), BF16...]
    unnamed x2 -> x0, blocking collectives: 67.3 us -> none
    dot_general x18 -> x0, matrix products: 66.3 us -> none  [the longest x1 15.9 us: on_device(): jnp.einsum('htk,ehk->the', key_low, key_cols, preferred_element_type=jnp....]
    another operation x2 -> x0, loops' own time: 62.3 us -> none  [carried_in(): return lax.fori_loop(0, length, hop, start)]
    reduce_scatter x1 -> x0, waiting for transfers between devices: 53.1 us -> none  [on_device(): lax.psum_scatter(term.astype(jnp.bfloat16), 'tp', scatter_dimension=0, ti...]
    select_n x64 -> x0, other arithmetic: 46.8 us -> none  [hop(): return jax.tree.map(lambda a, b: jnp.where(reached, a, b), new, before)]
    all_gather x2 -> x0, blocking collectives: 33.8 us -> none  [carried_in(): everything = jax.tree.map(lambda part: lax.all_gather(part, axis), shard)]
    dynamic_slice x32 -> x0, local copies, waits for them, and re-layouts: 20.3 us -> none  [hop(): new = combine(before, jax.tree.map(lambda part: part[at], everything))]
  transfers between devices with their start and end apart: 3 -> 0, of which waited for: 2 -> 0; matrix products, arithmetic and copies ran while one was open for 9% -> 0% of each run, Pallas kernels for 0% -> 0%
where the time goes in v1:
time: 85.5 us; the launch traced here: 85.4 us
  Pallas kernels  81.2 us (95%)
  local copies, waits for them, and re-layouts  3.48 us (4%)
    pallas_call x1, Pallas kernels, on_device(): pl.pallas_call(kernel, out_shape=(jax.ShapeDtypeStruct((OWN, WIDTH), BF16...  81.2 us
    unnamed x7, local copies, waits for them, and re-layouts  3.48 us

profile of v1, /device:TPU:1, one launch (start us, length us, event | category | flops | bytes accessed | tf_op | source)
XLA Modules:
  0.0 85.4 jit_solution(11072467178262433503)
XLA Ops:
  0.6 81.2 %shard_map.112 = (bf16[128,4096]{1,0:T(8,128)(2,1)}, f32[1,1024]{1,0:T(1,128)}, f32[1,1024]{1,0:T(1,128)}) custom-call(bf16[1024,256]{1,0:T(8,128)(2,1)} %q_hbm.1, bf16[1024,256]{1,0:T(8,128)(2,1)} %k_hbm.1, bf16[1024,512]{1,0:T(8,128)(2,1)} %v_hbm.1, bf16[1024,512]{1,0:T(8,128)(2,1)} %g_hbm.1, f32[1,1024]{1,0:T(1,128)} %in_ref.1, f32[1,1024]{1,0:T(1,128)} %forget_ref.1, ...), custom_call_target="tpu_custom_call" | custom-call | flops 16000000000 | bytes 13000000 | tf_op jit(solution)/shard_map/pallas_call | solution.py:461
  81.9 0.0 copy-start.1
  81.9 0.0 copy-start
  81.9 2.3 %copy.15 = bf16[128,4096]{1,0:T(8,128)(2,1)} copy(bf16[128,4096]{1,0:T(8,128)(2,1)} %get-tuple-element.6) | data formatting | bytes 2097152
  84.2 0.0 copy-done.1
  84.2 0.6 copy.16
  84.8 0.0 copy-done
  84.8 0.6 copy.17
Async XLA Ops:
  81.9 2.3 %copy-start.1 = (f32[1,1024]{1,0:T(1,128)S(1)}, f32[1,1024]{1,0:T(1,128)}, u32[]{:S(2)}) copy-start(f32[1,1024]{1,0:T(1,128)} %get-tuple-element.7) | copy-start | bytes 12292
  81.9 2.9 %copy-start = (f32[1,1024]{1,0:T(1,128)S(1)}, f32[1,1024]{1,0:T(1,128)}, u32[]{:S(2)}) copy-start(f32[1,1024]{1,0:T(1,128)} %get-tuple-element.8) | copy-start | bytes 12292

commit v2 on v1

v2 whole, which is shorter than its diff:
```python
import functools

import jax
import jax.numpy as jnp
from jax import lax
from jax.experimental import pallas as pl
from jax.experimental.pallas import tpu as pltpu
from jax.sharding import PartitionSpec as P

MESH = pl.DeviceIdType.MESH
HIGH = lax.Precision.HIGHEST
F32 = jnp.float32
BF16 = jnp.bfloat16
FLOOR = -1e30

TOK, DK, DV, WIDTH = 1024, 256, 512, 4096
BLOCKS = 16
PART = DK // BLOCKS
TILE = 256
TILES = TOK // TILE
COLS = 1024
HOPS = 12
SOON = DK + DV
FAR_FIRST = (10, 6, 14, 9, 11, 2, 8, 5, 7, 13, 15, 1, 3, 4, 12)
OWN = TOK // 8


def nn(a, b):
    return lax.dot_general(a, b, (((1,), (0,)), ((), ())), preferred_element_type=F32)


def nt(a, b):
    return lax.dot_general(a, b, (((1,), (1,)), ((), ())), preferred_element_type=F32)


def row_times(row, matrix):
    high = row.astype(BF16).astype(F32)
    middle = (row - high).astype(BF16).astype(F32)
    low = row - high - middle
    at = lax.broadcasted_iota(jnp.int32, (16, row.shape[1]), 0)
    pieces = jnp.where(at == 0, high, jnp.where(at == 1, middle, jnp.where(at == 2, low, 0.0)))
    return jnp.sum(nn(pieces.astype(BF16), matrix), axis=0, keepdims=True)


def halves(a):
    high = a.astype(BF16)
    return high, (a - high.astype(F32)).astype(BF16)


def twice(a):
    return jnp.concatenate([a, a], axis=1)


def kernel(
    q_hbm, k_hbm, v_hbm, g_hbm, in_hbm, forget_hbm, wq_hbm, wk_hbm, wv_hbm,
    token_ref, gate_grad_ref,
    q, k, v, g, in_ref, forget_ref, w_own, w_pair, q_t, k_t, weigh, pair, score_low, weight_low,
    near_query, near_key, near_value, stage, act_own, act_out, act_pair,
    fold, row_a, row_b, wide, reaching, wide_grad, stat, stat_back, stat_rx, stat_back_rx,
    fwd_a, fwd_b, fwd_peak, fwd_norm, bwd_a, bwd_b, bwd_peak, bwd_share,
    local, grad_state, rx_fwd, tx_fwd, before, rx_bwd, tx_bwd, after, after_high, after_low,
    product, own, tx_hop, rx_hop,
    load_sem, stat_send, stat_recv, part_send, part_recv, weight_send, weight_recv,
    act_send, act_recv, hop_send, hop_recv,
):
    ctx, tp = lax.axis_index("ctx"), lax.axis_index("tp")
    chip, core = lax.div(tp, 2), lax.rem(tp, 2)
    partner = 2 * chip + 1 - core

    def each_peer(do):
        for d in FAR_FIRST:
            do(lax.rem(ctx + d, BLOCKS))

    def neighbour(side):
        return 2 * lax.rem(chip + 1 + 2 * side, 4) + core

    loads = [
        pltpu.make_async_copy(source, target, load_sem.at[i])
        for i, (source, target) in enumerate(
            (
                (k_hbm, k),
                (v_hbm, v),
                (q_hbm, q),
                (g_hbm, g),
                (wq_hbm, w_own.at[:, pl.ds(0, DK)]),
                (wk_hbm, w_own.at[:, pl.ds(SOON, DK)]),
                (wv_hbm, w_own.at[:, pl.ds(DK, DV)]),
                (in_hbm, in_ref),
                (forget_hbm, forget_ref),
            )
        )
    ]
    for i in (8, 7, 0, 1, 2, 3):
        loads[i].start()

    barrier = pltpu.get_barrier_semaphore()
    each_peer(
        lambda p: pl.semaphore_signal(barrier, 1, device_id={"ctx": p}, device_id_type=MESH)
    )
    for other in (partner, neighbour(0), neighbour(1)):
        pl.semaphore_signal(barrier, 1, device_id={"tp": other}, device_id_type=MESH)

    loads[8].wait()
    loads[7].wait()

    def to_fold(row):
        for i in range(8):
            fold[i : i + 1, :] = row[:, 128 * i : 128 * i + 128]
        return fold[...]

    def to_row(folded, row_ref):
        fold[...] = folded
        for i in range(8):
            row_ref[:, 128 * i : 128 * i + 128] = fold[i : i + 1, :]
        return row_ref[...]

    lane = lax.broadcasted_iota(jnp.int32, (8, 128), 1)
    line = lax.broadcasted_iota(jnp.int32, (8, 128), 0)
    down = lax.broadcasted_iota(jnp.int32, (128, 128), 0)
    across = lax.broadcasted_iota(jnp.int32, (128, 128), 1)

    forget = forget_ref[...]
    small = jnp.exp(-jnp.abs(forget))
    series = small * (1.0 - small * (0.5 - small * (1.0 / 3.0 - small * 0.25)))
    log_forget = jnp.minimum(forget, 0.0) - jnp.where(
        small < 0.01, series, jnp.log(1.0 + small)
    )
    log_forget = to_fold(log_forget)
    inside = jnp.dot(
        log_forget, (down <= across).astype(F32), precision=HIGH, preferred_element_type=F32
    )
    lines = jnp.broadcast_to(inside[:, 127:128], (8, 128))
    for d in (1, 2, 4):
        lines = lines + jnp.where(line >= d, pltpu.roll(lines, d, 0), 0.0)
    cumulative = inside + jnp.where(line >= 1, pltpu.roll(lines, 1, 0), 0.0)
    total = lines[7:8, 0:1]
    level = to_fold(in_ref[...]) - cumulative
    top = jnp.max(jnp.max(level, axis=1, keepdims=True), axis=0, keepdims=True)
    first = level[0:1, 0:1]
    lift = jnp.exp(to_row(level, row_a) - top)

    loads[0].wait()
    def put_norm(tile, norm):
        tile[0:1, :] = norm[:, :128]
        tile[1:2, :] = norm[:, 128:]

    def norm_of(tile):
        return jnp.concatenate([tile[0:1, :], tile[1:2, :]], axis=1)

    stat[...] = jnp.zeros_like(stat)
    put_norm(stat, row_times(lift, k[...]))
    stat[2:3, :] = jnp.broadcast_to(total + top, (1, 128))
    stat[3:4, :] = jnp.broadcast_to(total, (1, 128))
    stat[4:5, :] = jnp.broadcast_to(first, (1, 128))

    def rows_of(ref, p):
        return ref.at[pl.ds(pl.multiple_of(p * PART, PART), PART)]

    def stat_copy(p, way, source, target, slot):
        return pltpu.make_async_remote_copy(
            src_ref=source, dst_ref=target.at[slot], send_sem=stat_send.at[way, p],
            recv_sem=stat_recv.at[way, slot], device_id={"ctx": p}, device_id_type=MESH,
        )

    def part_copy(p, way, source, target, slot):
        return pltpu.make_async_remote_copy(
            src_ref=source, dst_ref=target, send_sem=part_send.at[way, p],
            recv_sem=part_recv.at[way, slot], device_id={"ctx": p}, device_id_type=MESH,
        )

    def weight_copy(i):
        rows = pl.ds(pl.multiple_of(i * TOK, TOK), TOK)
        return pltpu.make_async_remote_copy(
            src_ref=w_own.at[rows], dst_ref=w_pair.at[rows], send_sem=weight_send.at[i],
            recv_sem=weight_recv.at[i], device_id={"tp": partner}, device_id_type=MESH,
        )

    pl.semaphore_wait(barrier, BLOCKS - 1 + 3)
    each_peer(lambda p: stat_copy(p, 0, stat, stat_rx, ctx).start())
    stat_rx[ctx] = stat[...]

    k_t[...] = k[...].T
    lifted_high, lifted_low = halves(k_t[...].astype(F32) * lift)
    loads[1].wait()
    local[...] = nn(lifted_high, v[...]) + nn(lifted_low, v[...])
    each_peer(lambda p: part_copy(p, 0, rows_of(local, p), rx_fwd.at[ctx], ctx).start())
    rx_fwd[ctx] = rows_of(local, ctx)[...]

    for load in loads[4:7]:
        load.start()

    highest = level
    for d in (1, 2, 4, 8, 16, 32, 64):
        highest = jnp.maximum(
            highest, jnp.where(lane >= d, pltpu.roll(highest, d, 1), FLOOR)
        )
    lines = jnp.broadcast_to(highest[:, 127:128], (8, 128))
    for d in (1, 2, 4):
        lines = jnp.maximum(lines, jnp.where(line >= d, pltpu.roll(lines, d, 0), FLOOR))
    highest = jnp.maximum(highest, jnp.where(line >= 1, pltpu.roll(lines, 1, 0), FLOOR))
    peak_row = to_row(highest, row_b)
    for i in range(8):
        wide[128 * i : 128 * i + 128, :] = jnp.broadcast_to(
            row_a[:, 128 * i : 128 * i + 128], (128, 128)
        ).T
    loads[2].wait()
    q_t[...] = q[...].T * jnp.asarray(0.0625, BF16)

    def span(i):
        return slice(TILE * i, TILE * (i + 1))

    causal = lax.broadcasted_iota(jnp.int32, (TILE, TILE), 0) <= lax.broadcasted_iota(
        jnp.int32, (TILE, TILE), 1
    )

    def damping_of(i, j):
        damping = jnp.exp(twice(wide[span(i), :]) - peak_row[:, span(j)])
        return jnp.where(causal, damping, 0.0) if i == j else damping

    def weigh_tiles(j):
        total_row = jnp.zeros((1, TILE), F32)
        for i in range(j + 1):
            weights = damping_of(i, j) * nn(k[span(i), :], q_t[:, span(j)])
            total_row = total_row + jnp.sum(weights, axis=0, keepdims=True)
            weigh[span(i), span(j)] = weights
        return total_row

    def pair_tiles(j):
        total_row = jnp.zeros((1, TILE), F32)
        for i in range(j + 1):
            pairs = nt(v[span(i), :], g[span(j), :])
            total_row = total_row + jnp.sum(
                weigh[span(i), span(j)] * pairs, axis=0, keepdims=True
            )
            pair[span(i), span(j)] = pairs
        return total_row

    weight_sum = jnp.concatenate([weigh_tiles(j) for j in range(TILES)], axis=1)
    loads[3].wait()
    pair_sums = [pair_tiles(0), pair_tiles(1)]
    for load in loads[4:7]:
        load.wait()
    lax.fori_loop(0, 4, lambda i, _: (weight_copy(i).start(), 0)[1], 0)

    each_peer(lambda p: stat_copy(p, 0, stat, stat_rx, p).wait_recv())
    peak = jnp.full((1, DK), FLOOR, F32)
    norm = jnp.zeros((1, DK), F32)
    for j in range(BLOCKS):
        fwd_peak[j] = peak
        fwd_norm[j] = norm
        shifted, highest_own = peak + twice(stat_rx[j, 3:4, :]), twice(stat_rx[j, 2:3, :])
        peak = jnp.maximum(shifted, highest_own)
        fwd_a[j] = jnp.exp(shifted - peak)
        fwd_b[j] = jnp.exp(highest_own - peak)
        norm = fwd_a[j] * norm + fwd_b[j] * norm_of(stat_rx[j])
    before_peak = fwd_peak[ctx][:, 0:1]
    before_norm = fwd_norm[ctx]
    stabilizer = jnp.maximum(peak_row, before_peak)
    shrunk = jnp.exp(peak_row - stabilizer)
    carried_scale = jnp.exp(before_peak - stabilizer)
    carried_norm = row_times(before_norm, q_t[...])
    denominator = weight_sum * shrunk + carried_scale * carried_norm
    square = denominator * denominator + 1.0
    inverse = 1.0 / jnp.sqrt(square)
    lifted_row = jnp.exp(stabilizer[:, 0:1] - stabilizer)
    lifted_high, lifted_low = halves(q_t[...].astype(F32) * (lifted_row * inverse))
    grad_state[...] = nn(lifted_high, g[...]) + nn(lifted_low, g[...])
    each_peer(lambda p: part_copy(p, 2, rows_of(grad_state, p), rx_bwd.at[ctx], ctx).start())
    rx_bwd[ctx] = rows_of(grad_state, ctx)[...]

    each_peer(lambda p: part_copy(p, 0, rows_of(local, p), rx_fwd.at[p], p).wait_recv())
    state = jnp.zeros((PART, DV), F32)
    for j in range(BLOCKS):
        tx_fwd[j] = state
        state = twice(fwd_a[j]) * state + twice(fwd_b[j]) * rx_fwd[j]
    each_peer(lambda p: part_copy(p, 1, tx_fwd.at[p], rows_of(before, ctx), ctx).start())
    rows_of(before, ctx)[...] = tx_fwd[ctx]

    peak = jnp.full((1, DK), FLOOR, F32)
    for j in reversed(range(BLOCKS)):
        bwd_peak[j] = peak
        highest_own = -jnp.maximum(twice(stat_rx[j, 4:5, :]), fwd_peak[j])
        shifted = peak + twice(stat_rx[j, 3:4, :])
        peak = jnp.maximum(shifted, highest_own)
        bwd_a[j] = jnp.exp(shifted - peak)
        bwd_b[j] = jnp.exp(highest_own - peak)
    after_peak = bwd_peak[ctx][:, 0:1]
    between = jnp.zeros((1, DK), F32)
    for j in range(BLOCKS):
        later = jnp.where(j > ctx, 1.0, 0.0)
        highest_own = -jnp.maximum(twice(stat_rx[j, 4:5, :]), fwd_peak[j])
        exponent = jnp.where(j > ctx, highest_own + between - after_peak, 0.0)
        bwd_share[j] = later * jnp.exp(exponent)
        between = between + later * twice(stat_rx[j, 3:4, :])
    reaching[...] = jnp.exp(wide[...] + (total + after_peak))

    pair_sums += [pair_tiles(2), pair_tiles(3)]
    pair_sum = jnp.concatenate(pair_sums, axis=1)

    each_peer(lambda p: part_copy(p, 2, rows_of(grad_state, p), rx_bwd.at[p], p).wait_recv())
    state = jnp.zeros((PART, DV), F32)
    for j in reversed(range(BLOCKS)):
        tx_bwd[j] = state
        state = twice(bwd_a[j]) * state + twice(bwd_b[j]) * rx_bwd[j]
    each_peer(lambda p: part_copy(p, 3, tx_bwd.at[p], rows_of(after, ctx), ctx).start())
    rows_of(after, ctx)[...] = tx_bwd[ctx]

    each_peer(lambda p: part_copy(p, 1, tx_fwd.at[p], rows_of(before, p), p).wait_recv())
    before_high, before_low = halves(before[...])
    back = nt(before_high, g[...]) + nt(before_low, g[...])
    q_wide = q_t[...].astype(F32)
    carried_pair = jnp.sum(back * q_wide, axis=0, keepdims=True)
    inner = (pair_sum * shrunk + carried_scale * carried_pair) * inverse
    grad_denominator = -inner * denominator / square
    stat_back[...] = jnp.zeros_like(stat_back)
    put_norm(stat_back, row_times(lifted_row * grad_denominator * 0.0625, q[...]))
    each_peer(lambda p: stat_copy(p, 1, stat_back, stat_back_rx, ctx).start())
    stat_back_rx[ctx] = stat_back[...]

    pair_scale = shrunk * inverse
    pair_shift = shrunk * grad_denominator
    for j in range(TILES):
        for i in range(j + 1):
            at = (span(i), span(j))
            score = damping_of(i, j) * (
                pair[at] * pair_scale[:, span(j)] + pair_shift[:, span(j)]
            )
            score_low[at] = score.astype(BF16)
            weight_low[at] = (weigh[at] * pair_scale[:, span(j)]).astype(BF16)

    norm_column = twice(jnp.broadcast_to(before_norm, (128, DK)).T)
    row_sums = []
    for j in range(TILES):
        near = nn(k_t[:, : TILE * (j + 1)], score_low[: TILE * (j + 1), span(j)])
        query_grad = near + carried_scale[:, span(j)] * (
            back[:, span(j)] * inverse[:, span(j)] + norm_column * grad_denominator[:, span(j)]
        )
        row_sums.append(jnp.sum(query_grad * q_wide[:, span(j)], axis=0, keepdims=True))
        near_query[span(j), :] = (query_grad * 0.0625).T.astype(BF16)
    row_grad = jnp.concatenate(row_sums, axis=1)
    for i in range(TILES):
        near_key[span(i), :] = nn(score_low[span(i), TILE * i :], q[TILE * i :, :]) * 0.0625
        near_value[span(i), :] = nn(weight_low[span(i), TILE * i :], g[TILE * i :, :])

    each_peer(lambda p: part_copy(p, 3, tx_bwd.at[p], rows_of(after, p), p).wait_recv())

    early, late = slice(0, SOON), slice(SOON, SOON + DK)

    def act_copy(slot, part):
        at = (pl.ds(slot * OWN, OWN), pl.ds(part.start, part.stop - part.start))
        sem = slot + 4 * (part.start > 0)
        return pltpu.make_async_remote_copy(
            src_ref=act_out.at[at], dst_ref=act_pair.at[at], send_sem=act_send.at[sem],
            recv_sem=act_recv.at[sem], device_id={"tp": partner}, device_id_type=MESH,
        )

    mine = pl.ds(pl.multiple_of(core * OWN, OWN), OWN)
    others = pl.ds(pl.multiple_of((1 - core) * OWN, OWN), OWN)
    hops = (2, 1, 3, 0)

    def tokens(slot):
        return pl.ds(
            pl.multiple_of(lax.rem(chip + hops[slot], 4) * 2 * OWN, 2 * OWN), 2 * OWN
        )

    def share(slot, part):
        rows = slice(slot * OWN, (slot + 1) * OWN)
        act_out[rows, part] = stage[others, part]
        act_copy(slot, part).start()
        act_own[rows, part] = stage[mine, part]

    def early_gradients(slot):
        rows = tokens(slot)
        reach = twice(twice(reaching[rows, :]))
        value_grad = near_value[rows, :] + reach * (
            nn(k[rows, :], after_high[...]) + nn(k[rows, :], after_low[...])
        )
        stage[:, 0:DK] = near_query[rows, :]
        stage[:, DK:SOON] = value_grad.astype(BF16)
        share(slot, early)
        return nt(v[rows, :], after_high[...]) + nt(v[rows, :], after_low[...])

    def late_gradients(slot, pulled):
        rows = tokens(slot)
        key_grad = near_key[rows, :] + twice(reaching[rows, :]) * (pulled + after_norm)
        stage[:, late] = key_grad.astype(BF16)
        share(slot, late)
        both = key_grad * k[rows, :].astype(F32)
        wide_grad[rows, :] = both[:, :128] + both[:, 128:]

    def hop_copy(s):
        return pltpu.make_async_remote_copy(
            src_ref=tx_hop.at[s], dst_ref=rx_hop.at[s], send_sem=hop_send.at[s],
            recv_sem=hop_recv.at[s], device_id={"tp": neighbour(lax.rem(s, 2))},
            device_id_type=MESH,
        )

    def columns(n):
        return pl.ds(pl.multiple_of(n * COLS, COLS), COLS)

    def multiply(act, weights, slot, n, part):
        rows = pl.ds(pl.multiple_of(slot * OWN, OWN), OWN)
        return nt(act[rows, part], weights[columns(n), part])

    def product_of(slot, n):
        whole = slice(0, SOON + DK)
        first_head = multiply(act_own, w_own, slot, n, whole)
        return first_head + multiply(act_pair, w_pair, slot, n, whole)

    def send(s, value):
        tx_hop[s] = value.astype(BF16)
        hop_copy(s).start()

    def nearest(s, _):
        side = lax.rem(s, 2)
        n = 2 * (1 - side) + lax.div(s - 4, 2)
        send(s, product_of(1 + side, n))
        return 0

    def join(s, _):
        side = lax.rem(s, 2)
        n = 2 * side + lax.div(s - 8, 2)
        product[...] = product_of(1 + side, n)
        hop_copy(s - 8).wait_recv()
        send(s, product[...] + rx_hop[s - 8].astype(F32))
        return 0

    def keep(n, _):
        own[:, columns(n)] = product_of(3, n)
        return 0

    def finish(i, _):
        half, part = lax.rem(i, 2), lax.div(i, 2)
        n = 2 * half + part
        from_left = 8 - 4 * half + 2 * part
        from_right = 5 + 4 * half + 2 * part
        hop_copy(from_left).wait_recv()
        hop_copy(from_right).wait_recv()
        both = rx_hop[from_left].astype(F32) + rx_hop[from_right].astype(F32)
        token_ref[:, columns(n)] = (own[:, columns(n)] + both).astype(BF16)
        return 0

    after_high[...], after_low[...] = halves(after[...])
    pulled = early_gradients(0)
    sums = [multiply(act_own, w_own, 0, n, early) for n in (0, 2)]
    lax.fori_loop(0, 4, lambda i, _: (weight_copy(i).wait_recv(), 0)[1], 0)

    each_peer(lambda p: stat_copy(p, 1, stat_back, stat_back_rx, p).wait_recv())
    after_norm = jnp.zeros((1, DK), F32)
    for j in range(BLOCKS):
        after_norm = after_norm + bwd_share[j] * norm_of(stat_back_rx[j])
    late_gradients(0, pulled)
    sums = [a + multiply(act_own, w_own, 0, n, late) for a, n in zip(sums, (0, 2))]
    act_copy(0, early).wait_recv()
    sums = [a + multiply(act_pair, w_pair, 0, n, early) for a, n in zip(sums, (0, 2))]
    act_copy(0, late).wait_recv()
    for s, n in ((0, 0), (1, 2)):
        send(s, sums[s] + multiply(act_pair, w_pair, 0, n, late))
    for s, n in ((2, 1), (3, 3)):
        send(s, product_of(0, n))
    for slot in (1, 2):
        late_gradients(slot, early_gradients(slot))
    for slot in (1, 2):
        act_copy(slot, early).wait_recv()
        act_copy(slot, late).wait_recv()
    lax.fori_loop(4, 8, nearest, 0)
    late_gradients(3, early_gradients(3))
    lax.fori_loop(8, 12, join, 0)
    act_copy(3, early).wait_recv()
    act_copy(3, late).wait_recv()
    lax.fori_loop(0, 4, keep, 0)

    in_grad_ref, forget_grad_ref = gate_grad_ref.at[0:1], gate_grad_ref.at[1:2]

    for i in range(8):
        in_grad_ref[:, 128 * i : 128 * i + 128] = jnp.sum(
            wide_grad[128 * i : 128 * i + 128, :].T, axis=0, keepdims=True
        )
    end_a, end_b = fwd_a[ctx][:, 0:1], fwd_b[ctx][:, 0:1]
    end_state = end_a * before[...] + end_b * local[...]
    end_norm = end_a * before_norm + end_b * norm_of(stat[...])
    linked = jnp.sum(
        jnp.sum(end_state * after[...], axis=1, keepdims=True), axis=0, keepdims=True
    ) + jnp.sum(end_norm * after_norm, axis=1, keepdims=True)
    end_peak = jnp.maximum(before_peak + total, total + top)
    link = jnp.exp(end_peak + after_peak) * linked
    balance = to_fold(row_grad - in_grad_ref[...])
    inside = jnp.dot(
        balance, (down >= across).astype(F32), precision=HIGH, preferred_element_type=F32
    )
    lines = jnp.broadcast_to(inside[:, 0:1], (8, 128))
    for d in (1, 2, 4):
        lines = lines + jnp.where(line < 8 - d, pltpu.roll(lines, 8 - d, 0), 0.0)
    later_sum = inside + jnp.where(line < 7, pltpu.roll(lines, 7, 0), 0.0)
    forget_grad_ref[...] = (to_row(later_sum, row_a) + link) / (1.0 + jnp.exp(forget))

    lax.fori_loop(0, 4, finish, 0)

    def sent(p):
        for way, (source, target) in enumerate(((stat, stat_rx), (stat_back, stat_back_rx))):
            stat_copy(p, way, source, target, ctx).wait_send()
        part_copy(p, 0, rows_of(local, p), rx_fwd.at[ctx], ctx).wait_send()
        part_copy(p, 1, tx_fwd.at[p], rows_of(before, ctx), ctx).wait_send()
        part_copy(p, 2, rows_of(grad_state, p), rx_bwd.at[ctx], ctx).wait_send()
        part_copy(p, 3, tx_bwd.at[p], rows_of(after, ctx), ctx).wait_send()

    each_peer(sent)
    lax.fori_loop(0, 4, lambda i, _: (weight_copy(i).wait_send(), 0)[1], 0)
    for slot in range(4):
        act_copy(slot, early).wait_send()
        act_copy(slot, late).wait_send()
    lax.fori_loop(0, HOPS, lambda s, _: (hop_copy(s).wait_send(), 0)[1], 0)


def on_device(*arrays):
    vm = pltpu.VMEM
    dma = pltpu.SemaphoreType.DMA
    anywhere = pl.BlockSpec(memory_space=pl.ANY)
    depth = 2 * DK + DV
    scratch = [
        vm((TOK, DK), BF16), vm((TOK, DK), BF16), vm((TOK, DV), BF16), vm((TOK, DV), BF16),
        vm((1, TOK), F32), vm((1, TOK), F32),
        vm((WIDTH, depth), BF16), vm((WIDTH, depth), BF16),
        vm((DK, TOK), BF16), vm((DK, TOK), BF16),
        vm((TOK, TOK), F32), vm((TOK, TOK), F32), vm((TOK, TOK), BF16), vm((TOK, TOK), BF16),
        vm((TOK, DK), BF16), vm((TOK, DK), F32), vm((TOK, DV), F32), vm((2 * OWN, depth), BF16),
        vm((4 * OWN, depth), BF16), vm((4 * OWN, depth), BF16), vm((4 * OWN, depth), BF16),
        vm((8, 128), F32), vm((1, TOK), F32), vm((1, TOK), F32),
        vm((TOK, 128), F32), vm((TOK, 128), F32), vm((TOK, 128), F32),
        vm((8, 128), F32), vm((8, 128), F32), vm((BLOCKS, 8, 128), F32), vm((BLOCKS, 8, 128), F32),
        *[vm((BLOCKS, 1, DK), F32) for _ in range(8)],
        vm((DK, DV), F32), vm((DK, DV), F32),
        vm((BLOCKS, PART, DV), F32), vm((BLOCKS, PART, DV), F32), vm((DK, DV), F32),
        vm((BLOCKS, PART, DV), F32), vm((BLOCKS, PART, DV), F32), vm((DK, DV), F32),
        vm((DK, DV), BF16), vm((DK, DV), BF16),
        vm((OWN, COLS), F32), vm((OWN, WIDTH), F32),
        vm((HOPS, OWN, COLS), BF16), vm((HOPS, OWN, COLS), BF16),
        dma((9,)), dma((2, BLOCKS)), dma((2, BLOCKS)), dma((4, BLOCKS)), dma((4, BLOCKS)),
        dma((4,)), dma((4,)), dma((8,)), dma((8,)), dma((HOPS,)), dma((HOPS,)),
    ]
    shapes = (
        jax.ShapeDtypeStruct((OWN, WIDTH), BF16),
        jax.ShapeDtypeStruct((2, TOK), F32),
    )
    token_grad, gate_grads = pl.pallas_call(
        kernel,
        out_shape=tuple(pltpu.VMEM(a.shape, a.dtype) for a in shapes),
        in_specs=[anywhere] * 9,
        scratch_shapes=scratch,
        compiler_params=pltpu.CompilerParams(
            collective_id=0, has_side_effects=True, vmem_limit_bytes=60 * 1024 * 1024
        ),
        cost_estimate=pl.CostEstimate(
            flops=16_000_000_000, bytes_accessed=13_000_000, transcendentals=1_000_000
        ),
    )(*arrays)
    return token_grad, gate_grads[0:1], gate_grads[1:2]


def solution(mesh):
    block = P("ctx", "tp")
    gate = P("tp", "ctx")
    weight = P(None, "tp")
    return jax.shard_map(
        on_device,
        mesh=mesh,
        in_specs=(block, block, block, block, gate, gate, weight, weight, weight),
        out_specs=(P(("ctx", "tp"), None), gate, gate),
        check_vma=False,
    )
```

time: 85.5 us -> 80.2 us (0.938)
  Pallas kernels: 81.2 us -> 77.2 us
  local copies, waits for them, and re-layouts: 3.48 us -> 1.58 us
    pallas_call x1, Pallas kernels: 81.2 us -> 77.2 us  [on_device(): pl.pallas_call(kernel, out_shape=tuple((pltpu.VMEM(a.shape, a.dtype) for...]
    unnamed x7 -> x1, local copies, waits for them, and re-layouts: 3.48 us -> 0.97 us
where the time goes in v2:
time: 80.2 us; the launch traced here: 79.4 us
  Pallas kernels  77.2 us (96%)
  local copies, waits for them, and re-layouts  1.58 us (2%)
    pallas_call x1, Pallas kernels, on_device(): pl.pallas_call(kernel, out_shape=tuple((pltpu.VMEM(a.shape, a.dtype) for...  77.2 us

profile of v2, /device:TPU:1, one launch (start us, length us, event | category | flops | bytes accessed | tf_op | source)
XLA Modules:
  0.0 79.4 jit_solution(17406592916533721228)
XLA Ops:
  0.6 77.2 %shard_map.112 = (bf16[128,4096]{1,0:T(8,128)(2,1)S(1)}, f32[2,1024]{1,0:T(2,128)S(1)}) custom-call(bf16[1024,256]{1,0:T(8,128)(2,1)} %q_hbm.1, bf16[1024,256]{1,0:T(8,128)(2,1)} %k_hbm.1, bf16[1024,512]{1,0:T(8,128)(2,1)} %v_hbm.1, bf16[1024,512]{1,0:T(8,128)(2,1)} %g_hbm.1, f32[1,1024]{1,0:T(1,128)} %in_hbm.1, f32[1,1024]{1,0:T(1,128)} %forget_hbm.1, ...), custom_call_target="tpu_custom_call" | custom-call | flops 16000000000 | bytes 13000000 | tf_op jit(solution)/shard_map/pallas_call | solution.py:545
  77.9 1.0 %copy.13 = bf16[128,4096]{1,0:T(8,128)(2,1)} copy(bf16[128,4096]{1,0:T(8,128)(2,1)S(1)} %get-tuple-element.9) | data formatting | bytes 2097152
  78.8 0.6 fusion
